TPU v7x, 32 devices: a whole 2x2x4 slice. The times are simulated.
32 devices in a mesh: depth: 16 (over z, x, core), az: 2 (over y).
Axes of the slice: x: 2, y: 2, z: 4, core: 2. Of those that a mesh axis runs over, the one named last changes fastest.
Arguments:
- velocity: float32 [6, 256, 64, 128], P(None, 'depth', 'az'), may hold values from -6 to 6
- stress: float32 [7, 256, 64, 128], P(None, 'depth', 'az'), may hold values from -6 to 6
- memory: float32 [12, 256, 64, 128], P(None, 'depth', 'az'), may hold values from -3 to 3
- layer_ids: int32 [64, 32], P('depth'), may hold values from 0 to 7, as said below
- materials: float32 [8, 8], replicated, may hold values from 0.006 to 4, as said below
- jkd: float32 [8, 9], replicated, may hold values from 0.1 to 60, as said below
- source_depth: int32 [1], replicated, may hold values from 0 to 255
Outputs:
- velocity_out: float32 [6, 256, 64, 128], P(None, 'depth', 'az')
- stress_out: float32 [7, 256, 64, 128], P(None, 'depth', 'az')
- memory_out: float32 [12, 256, 64, 128], P(None, 'depth', 'az')
Inputs may be any that keep to these rules, and one draw needn't show every extreme that they name: `layer_ids`: the first 4 radial elements hold 0 (borehole fluid); beyond them each depth element holds one formation row of 1 to 7 for all its radial elements. `materials`: columns: lambda0 0.5 to 1.5, shear modulus 0.3 to 1 (row 0: 0.006 to 0.02), M 0.5 to 1.5, beta 0.3 to 0.9, bulk density 1.5 to 2.5, fluid density 0.8 to 1.2, tortuosity 1.5 to 4, friction 0.5 to 2. `jkd`: omega 0.5 to 5, pole weights 0.1 to 1, pole rates 0.3 to 60.
All inputs are finite; a program needn't handle non-finite values.
Results may differ from a plain program's by a relative error of at most 0.0001.
Values sent between devices are 32-bit elements; how exact they have to be, the bound alone decides.
A program may use at most 128 MiB of HBM per device.

v0:
```python
import functools
import math

import jax
import jax.numpy as jnp
import numpy as np
from jax import lax
from jax.experimental import pallas as pl
from jax.experimental.pallas import tpu as pltpu
from jax.sharding import PartitionSpec as P

STEPS = 2
RB = 4


DT = 0.02
SOURCE_GAIN = 40.0
R_INNER = 1.0
MESH = pl.DeviceIdType.MESH
F32 = jnp.float32
BF16 = jnp.bfloat16


def gll_basis():
    root_value = math.sqrt(3.0 / 7.0)
    gll_nodes = np.array([-1.0, -root_value, 0.0, root_value, 1.0])
    weights = np.array([0.1, 49.0 / 90.0, 32.0 / 45.0, 49.0 / 90.0, 0.1])
    offsets = gll_nodes[:, None] - gll_nodes[None, :] + np.eye(5)
    factors = np.prod(offsets, axis=1)
    derivative = factors[:, None] / factors[None, :] / offsets
    diagonal_part = np.sum(1.0 / offsets, axis=1) - 1.0
    derivative = derivative * (1.0 - np.eye(5)) + np.eye(5) * diagonal_part[:, None]
    return (gll_nodes, weights, derivative)


def radial_operator(node_count):
    gll_nodes, weights, derivative = gll_basis()
    full_count = node_count + 1
    stencil = weights[:, None] * derivative * 2.0
    assembled = np.zeros((full_count, full_count))
    node_mass = np.zeros(full_count)
    for element in range(node_count // 4):
        assembled[4 * element : 4 * element + 5, 4 * element : 4 * element + 5] += stencil
        node_mass[4 * element : 4 * element + 5] += weights
    return (assembled / node_mass[:, None])[:node_count, :node_count]


def radial_positions(node_count):
    gll_nodes, weights, derivative = gll_basis()
    positions = np.arange(node_count)
    return R_INNER + positions // 4 + 0.5 * (1.0 + gll_nodes[positions % 4])


def azimuth_operator(node_count):
    positions = np.arange(node_count)
    offsets = positions[:, None] - positions[None, :]
    wave_modes = np.arange(1, node_count // 2)
    phases = 2.0 * np.pi * offsets[:, :, None] * wave_modes[None, None, :] / node_count
    return -(2.0 / node_count) * np.sum(wave_modes * np.sin(phases), axis=2)


def split_high_low(matrix):
    matrix = np.asarray(matrix, np.float32)
    high = matrix.astype(jnp.bfloat16)
    low = (matrix - high.astype(np.float32)).astype(jnp.bfloat16)
    return high, low


A1, A2, A3, FA, OM, INV, LF, BM, MU, PM, NCOEF = 0, 1, 2, 3, 7, 8, 12, 13, 14, 15, 16


def weighted(terms):
    total = None
    for factor, value in terms:
        if abs(factor) < 1e-12:
            continue
        term = value * np.float32(factor)
        total = term if total is None else total + term
    return total


def step_kernel(
    depth_devices, az_devices,
    source, mats_in, jkd_in, ids_in, expand_in, radial_in, azim_in, inv_r_in, vel_in, str_in, mem_in,
    vel_out, str_out, mem,
    mats, jkd, ids, expand, radial_k, azim_k, inv_r,
    s_az, s_rest, v_az, v_rest, far_s, far_v, far_new, far_dw, far_psi, far_dt, dw, psi_t,
    halo_above, halo_below, far_above, far_below, up_stage, down_stage,
    partial, far_partial, coef, rad_d, az_d,
    load_sem, store_sem, az_send, az_recv, up_send, up_recv, down_send, down_recv,
):
    me_d = lax.axis_index("depth")
    me_a = lax.axis_index("az")
    depth, azims, radii = mem.shape[1:]
    chunks = depth // 4
    others = range(az_devices - 1)
    has_up = me_d < depth_devices - 1
    has_down = me_d > 0
    _, weights, derivative = gll_basis()
    stencil = weights[:, None] * derivative * 2.0

    inner = pl.ds(0, depth)
    stress_place = [(s_rest, 0), (s_az, 1), (s_rest, 1), (s_az, 0), (s_rest, 2), (s_az, 2), (s_az, 3)]
    vel_place = [(v_az, 0), (v_az, 2), (v_az, 1), (v_rest, 0), (v_az, 3), (v_rest, 1)]
    pairs = [(str_in.at[i], ref.at[k, inner]) for i, (ref, k) in enumerate(stress_place)]
    pairs += [(vel_in.at[i], ref.at[k, inner]) for i, (ref, k) in enumerate(vel_place)]
    pairs += [(mem_in, mem), (mats_in, mats), (jkd_in, jkd), (ids_in, ids), (expand_in, expand)]
    pairs += [(radial_in, radial_k), (azim_in, azim_k), (inv_r_in, inv_r)]
    loads = [
        pltpu.make_async_copy(src, dst, load_sem.at[i]) for i, (src, dst) in enumerate(pairs)
    ]
    for index in (1, 3, 5, 6, 14, 15, 16, 17, 0, 2, 4, 18, 19, 20, 7, 8, 9, 10, 11, 12, 13):
        loads[index].start()

    def other_az(k, sign):
        return lax.rem(me_a + (az_devices + sign * k), az_devices)

    barrier = pltpu.get_barrier_semaphore()

    def greet(where_d, where_a):
        pl.semaphore_signal(barrier, inc=1, device_id=(where_d, where_a), device_id_type=MESH)

    for k in range(1, az_devices):
        greet(me_d, other_az(k, 1))

    @pl.when(has_up)
    def _():
        for k in range(az_devices):
            greet(me_d + 1, other_az(k, 1))

    @pl.when(has_down)
    def _():
        for k in range(az_devices):
            greet(me_d - 1, other_az(k, 1))

    neighbours = has_up.astype(jnp.int32) + has_down.astype(jnp.int32)
    pl.semaphore_wait(barrier, (az_devices - 1) + az_devices * neighbours)

    exchanges = [
        (s_az, far_s, 4), (v_az, far_v, 4), (psi_t, far_psi, 1), (dw, far_dw, 1), (v_az, far_new, 2),
    ]

    def az_copies(which, e):
        source_ref, target_ref, count = exchanges[which]
        planes = pl.ds(pl.multiple_of(4 * e, 4), 4)
        return [
            pltpu.make_async_remote_copy(
                src_ref=source_ref.at[pl.ds(0, count), planes],
                dst_ref=target_ref.at[k, pl.ds(0, count), planes],
                send_sem=az_send.at[which, k, e],
                recv_sem=az_recv.at[which, k, e],
                device_id=(me_d, other_az(k + 1, -1)),
                device_id_type=MESH,
            )
            for k in others
        ]

    def start_az(which, e):
        for copy in az_copies(which, e):
            copy.start()

    def receive_az(which, e):
        for copy in az_copies(which, e):
            copy.wait_recv()

    far_fields = {1: (1, 2), 2: (1, 1)}

    def halo_copies(half, stage, near, far, send_sem, recv_sem, where_d):
        copies = [
            pltpu.make_async_remote_copy(
                src_ref=stage.at[half], dst_ref=near.at[half],
                send_sem=send_sem.at[half, 0], recv_sem=recv_sem.at[half, 0],
                device_id=(where_d, me_a), device_id_type=MESH,
            )
        ]
        if half in far_fields:
            first, count = far_fields[half]
            for k in others:
                copies.append(
                    pltpu.make_async_remote_copy(
                        src_ref=stage.at[half, pl.ds(first, count)],
                        dst_ref=far.at[half - 1, k, pl.ds(0, count)],
                        send_sem=send_sem.at[half, k + 1], recv_sem=recv_sem.at[half, k + 1],
                        device_id=(where_d, other_az(k + 1, -1)), device_id_type=MESH,
                    )
                )
        return copies

    def up_copies(half):
        return halo_copies(half, up_stage, halo_below, far_below, up_send, up_recv, me_d + 1)

    def down_copies(half):
        return halo_copies(half, down_stage, halo_above, far_above, down_send, down_recv, me_d - 1)

    stress_dz = [(s_rest, 2), (s_az, 2), (s_rest, 1), (s_az, 3)]
    vel_dz = [(v_az, 0), (v_az, 1), (v_az, 2), (v_rest, 1)]

    def top_of(read, base):
        return weighted([(stencil[4, l], read(base + l)) for l in range(4)])

    def bottom_of(read):
        return weighted([(stencil[0, l] * (2.0 if l == 0 else 1.0), read(l)) for l in range(5)])

    def reader(ref, k):
        return lambda z: ref[k, z]

    def far_reader(ref, k, f):
        return lambda z: ref[k, f, z]

    def send_down(half, dz_fields):
        for f, (ref, k) in enumerate(dz_fields):
            down_stage[half, f] = ref[k, 0]

        @pl.when(has_down)
        def _():
            for copy in down_copies(half):
                copy.start()

    def send_up(half, dz_fields):
        for f, (ref, k) in enumerate(dz_fields):
            up_stage[half, f] = top_of(reader(ref, k), depth - 4)

        @pl.when(has_up)
        def _():
            for copy in up_copies(half):
                copy.start()

    def receive_halos(half, dz_fields):
        for e in range(1, chunks):
            for f, (ref, k) in enumerate(dz_fields):
                partial[f, e] = top_of(reader(ref, k), 4 * (e - 1))

        @pl.when(has_up)
        def _():
            down_copies(half)[0].wait_recv()
            for f, (ref, k) in enumerate(dz_fields):
                ref[k, depth] = halo_above[half, f]

        @pl.when(jnp.logical_not(has_up))
        def _():
            for f, (ref, k) in enumerate(dz_fields):
                ref[k, depth] = jnp.zeros((azims, radii), F32)

        @pl.when(has_down)
        def _():
            up_copies(half)[0].wait_recv()
            partial[:, 0] = halo_below[half]

        @pl.when(jnp.logical_not(has_down))
        def _():
            for f, (ref, k) in enumerate(dz_fields):
                partial[f, 0] = bottom_of(reader(ref, k))

    def receive_far_halos(half, ref):
        first, count = far_fields[half]
        fields = [(k, i, FAR_DZ[half][i]) for k in others for i in range(count)]
        for e in range(1, chunks):
            for k, i, f in fields:
                far_partial[k, i, e] = top_of(far_reader(ref, k, f), 4 * (e - 1))

        @pl.when(has_up)
        def _():
            for copy in down_copies(half)[1:]:
                copy.wait_recv()
            for k, i, f in fields:
                ref[k, f, depth] = far_above[half - 1, k, i]

        @pl.when(jnp.logical_not(has_up))
        def _():
            for k, i, f in fields:
                ref[k, f, depth] = jnp.zeros((azims, radii), F32)

        @pl.when(has_down)
        def _():
            for copy in up_copies(half)[1:]:
                copy.wait_recv()
            for k, i, f in fields:
                far_partial[k, i, 0] = far_below[half - 1, k, i]

        @pl.when(jnp.logical_not(has_down))
        def _():
            for k, i, f in fields:
                far_partial[k, i, 0] = bottom_of(far_reader(ref, k, f))

    def finish_az(which):
        for e in range(chunks):
            for copy in az_copies(which, e):
                copy.wait_send()

    def finish_halos(half):
        @pl.when(has_up)
        def _():
            for copy in up_copies(half):
                copy.wait_send()

        @pl.when(has_down)
        def _():
            for copy in down_copies(half):
                copy.wait_send()

    def dz_at(read, below, base, j):
        if j == 0:
            total = weighted([(stencil[0, l], read(base + l)) for l in range(1, 5)])
            return (total + below) * np.float32(1.0 / (2.0 * weights[0]))
        return weighted([(2.0 * derivative[j, l], read(base + l)) for l in range(5)])

    def high_low(value, axis):
        high = value.astype(BF16)
        low = (value - high.astype(F32)).astype(BF16)
        return jnp.concatenate([high, low, high], axis=axis)

    def radial_part(blocks):
        rows = jnp.concatenate([block.reshape(4 * azims, radii) for block in blocks], axis=0)
        result = jnp.dot(high_low(rows, 1), radial_k[...], preferred_element_type=F32)
        rad_d[0 : len(blocks)] = result.reshape(len(blocks), 4, azims, radii)

    def azimuth_part(near, far, base, kept):
        rows = azims * az_devices if kept else azims
        for j in range(4):
            blocks = [jnp.concatenate([ref[f, base + j] for ref, f in near], axis=1)]
            for k in others:
                blocks.append(jnp.concatenate([ref[k, f, base + j] for ref, f in far], axis=1))
            column = jnp.concatenate(blocks, axis=0)
            result = jnp.dot(
                azim_k[0:rows, :], high_low(column, 0), preferred_element_type=F32
            )
            az_d[j] = result[0:azims]
            for i, f in enumerate(kept):
                for k in others:
                    far_dt[k, i, base + j] = result[
                        (k + 1) * azims : (k + 2) * azims, f * radii : (f + 1) * radii
                    ]

    def az_at(j, f):
        return az_d[j, :, f * radii : (f + 1) * radii]

    def row_of(e):
        def row(index):
            return coef[index, pl.ds(e, 1), :]

        return row

    def shot_at(step, z):
        gain = np.float32(DT * SOURCE_GAIN * math.cos(0.9 * step))
        lane = lax.broadcasted_iota(jnp.int32, (1, radii), 1)
        wanted = jnp.zeros((1, radii), jnp.int32) + source[0]
        return jnp.where((wanted == me_d * depth + z) & (lane < 4 * RB), gain, np.float32(0.0))

    def velocity_chunk(step, e):
        base = pl.multiple_of(4 * e, 4)
        planes = pl.ds(base, 4)
        row = row_of(e)
        if step == 0:
            receive_az(0, e)
        else:
            receive_az(3, e)
            for k in others:
                for j in range(4):
                    z = base + j
                    far_s[k, 1, z] = far_s[k, 1, z] + row(BM) * far_dw[k, 0, z]
                    far_s[k, 3, z] = far_s[k, 3, z] - row(PM) * far_dw[k, 0, z]
        radial_part([s_rest[0, planes], s_az[0, planes], s_rest[2, planes], s_az[3, planes]])
        azimuth_part(
            [(s_az, f) for f in range(4)], [(far_s, f) for f in range(4)], base,
            (1, 3) if step == 1 else (),
        )
        q = inv_r[...]
        for j in range(4):
            z = base + j
            rt, tt = s_az[0, z], s_az[1, z]
            rr, rz = s_rest[0, z], s_rest[2, z]
            dz = [
                dz_at(reader(ref, k), partial[f, e], base, j)
                for f, (ref, k) in enumerate(stress_dz)
            ]
            div = [
                rad_d[0, j] + q * (az_at(j, 0) + (rr - tt)) + dz[0],
                rad_d[1, j] + q * (az_at(j, 1) + 2.0 * rt) + dz[1],
                rad_d[2, j] + q * (az_at(j, 2) + rz) + dz[2],
            ]
            grad = [rad_d[3, j], q * az_at(j, 3), dz[3]]
            solid = [(v_az, 0), (v_az, 2), (v_az, 1)]
            fluid = [(v_rest, 0), (v_az, 3), (v_rest, 1)]
            for c in range(3):
                psi = [mem[3 * pole + c, z] for pole in range(4)]
                resist = grad[c]
                for pole in range(4):
                    resist = resist + row(FA + pole) * psi[pole]
                ref, k = solid[c]
                ref[k, z] = ref[k, z] + (row(A1) * div[c] + row(A2) * resist)
                change = -(row(A2) * div[c] + row(A3) * resist)
                ref, k = fluid[c]
                fresh = ref[k, z] + change
                ref[k, z] = fresh
                change = change + row(OM) * fresh
                psi = [(psi[pole] + change) * row(INV + pole) for pole in range(4)]
                for pole in range(4):
                    mem[3 * pole + c, z] = psi[pole]
                if c == 1 and step == 0:
                    total = row(FA) * psi[0]
                    for pole in range(1, 4):
                        total = total + row(FA + pole) * psi[pole]
                    psi_t[0, z] = total

    def stress_chunk(step, e):
        base = pl.multiple_of(4 * e, 4)
        planes = pl.ds(base, 4)
        radial_part([v_az[0, planes], v_az[2, planes], v_az[1, planes], v_rest[0, planes]])
        if step == 0:
            receive_az(1, e)
            far = [(far_v, f) for f in range(4)]
        else:
            receive_az(4, e)
            far = [(far_new, 0), (far_new, 1), (far_v, 2), (far_v, 3)]
        azimuth_part([(v_az, f) for f in range(4)], far, base, (0, 1, 2) if step == 0 else ())
        row = row_of(e)
        q = inv_r[...]
        for j in range(4):
            z = base + j
            vr, vt, wr = v_az[0, z], v_az[2, z], v_rest[0, z]
            dz = [
                dz_at(reader(ref, k), partial[f, e], base, j)
                for f, (ref, k) in enumerate(vel_dz)
            ]
            e_rr = rad_d[0, j]
            e_tt = q * (vr + az_at(j, 2))
            e_zz = dz[1]
            g_rt = q * (az_at(j, 0) - vt) + rad_d[1, j]
            g_rz = dz[0] + rad_d[2, j]
            g_tz = dz[2] + q * az_at(j, 1)
            div_v = e_rr + e_tt + e_zz
            div_w = rad_d[3, j] + q * (wr + az_at(j, 3)) + dz[3]
            if step == 0:
                dw[0, z] = div_w
            bulk = row(LF) * div_v + row(BM) * div_w
            twice = 2.0 * row(MU)
            s_rest[0, z] = s_rest[0, z] + (bulk + twice * e_rr)
            s_az[1, z] = s_az[1, z] + (bulk + twice * e_tt)
            s_rest[1, z] = s_rest[1, z] + (bulk + twice * e_zz)
            s_az[0, z] = s_az[0, z] + row(MU) * g_rt
            s_rest[2, z] = s_rest[2, z] + row(MU) * g_rz
            s_az[2, z] = s_az[2, z] + row(MU) * g_tz
            s_az[3, z] = s_az[3, z] - (row(BM) * div_v + row(PM) * div_w) + shot_at(step, z)

    def far_stress_chunk(e):
        base = pl.multiple_of(4 * e, 4)
        planes = pl.ds(base, 4)
        row = row_of(e)
        q = inv_r[...]
        for k in others:
            radial_part([far_v[k, 0, planes], far_v[k, 2, planes]])
            for j in range(4):
                z = base + j
                vr, vt = far_v[k, 0, z], far_v[k, 2, z]
                dz_vz = dz_at(far_reader(far_v, k, 1), far_partial[k, 0, e], base, j)
                dz_vt = dz_at(far_reader(far_v, k, 2), far_partial[k, 1, e], base, j)
                e_tt = q * (vr + far_dt[k, 2, z])
                div_v = rad_d[0, j] + e_tt + dz_vz
                g_rt = q * (far_dt[k, 0, z] - vt) + rad_d[1, j]
                g_tz = dz_vt + q * far_dt[k, 1, z]
                far_s[k, 0, z] = far_s[k, 0, z] + row(MU) * g_rt
                far_s[k, 1, z] = far_s[k, 1, z] + (row(LF) * div_v + 2.0 * row(MU) * e_tt)
                far_s[k, 2, z] = far_s[k, 2, z] + row(MU) * g_tz
                far_s[k, 3, z] = far_s[k, 3, z] - row(BM) * div_v + shot_at(0, z)

    def far_velocity_chunk(e):
        base = pl.multiple_of(4 * e, 4)
        planes = pl.ds(base, 4)
        row = row_of(e)
        q = inv_r[...]
        receive_az(2, e)
        for k in others:
            radial_part([far_s[k, 0, planes]])
            for j in range(4):
                z = base + j
                dz_tz = dz_at(far_reader(far_s, k, 2), far_partial[k, 0, e], base, j)
                div = rad_d[0, j] + q * (far_dt[k, 0, z] + 2.0 * far_s[k, 0, z]) + dz_tz
                resist = q * far_dt[k, 1, z] + far_psi[k, 0, z]
                far_v[k, 2, z] = far_v[k, 2, z] + (row(A1) * div + row(A2) * resist)
                far_v[k, 3, z] = far_v[k, 3, z] - (row(A2) * div + row(A3) * resist)

    def each_chunk(body):
        def wrapped(e, carry):
            body(e)
            return carry

        lax.fori_loop(0, chunks, wrapped, 0)

    for index in (1, 3, 5, 6):
        loads[index].wait()
    for e in range(chunks):
        start_az(0, e)
    for index in (0, 2, 4):
        loads[index].wait()
    send_down(0, stress_dz)
    send_up(0, stress_dz)
    for index in range(14, 21):
        loads[index].wait()

    ids_node = jnp.dot(
        ids[...].astype(F32).astype(BF16), expand[...], preferred_element_type=F32
    )

    def pick(table, column):
        value = jnp.zeros_like(ids_node)
        for r in range(8):
            value = jnp.where(ids_node == float(r), table[r : r + 1, column : column + 1], value)
        return value

    lame_zero, shear, modulus, coupling, rho, rho_f, tort, fric = [pick(mats, c) for c in range(8)]
    omega = pick(jkd, 0)
    rho_w = rho_f * tort
    scale = DT / (rho * rho_w - rho_f * rho_f)
    coef[A1] = rho_w * scale
    coef[A2] = rho_f * scale
    coef[A3] = rho * scale
    for pole in range(4):
        coef[FA + pole] = fric * pick(jkd, 1 + pole)
        coef[INV + pole] = 1.0 / (1.0 + DT * (pick(jkd, 5 + pole) + omega))
    coef[OM] = DT * omega
    coef[LF] = DT * (lame_zero + coupling * coupling * modulus)
    coef[BM] = DT * coupling * modulus
    coef[MU] = DT * shear
    coef[PM] = DT * modulus

    for index in range(7, 14):
        loads[index].wait()

    stores = []

    def to_out(src, dst):
        copy = pltpu.make_async_copy(src, dst, store_sem.at[len(stores)])
        copy.start()
        stores.append(copy)

    receive_halos(0, stress_dz)

    def first_velocity(e):
        velocity_chunk(0, e)
        start_az(1, e)

        @pl.when(e == 0)
        def _():
            send_down(1, vel_dz)

    each_chunk(first_velocity)
    send_up(1, vel_dz)
    for e in range(chunks):
        start_az(2, e)
    finish_az(0)
    finish_halos(0)

    receive_halos(1, vel_dz)

    def first_stress(e):
        stress_chunk(0, e)
        start_az(3, e)

        @pl.when(e == 0)
        def _():
            send_down(2, stress_dz)

    each_chunk(first_stress)
    send_up(2, stress_dz)
    receive_far_halos(1, far_v)
    each_chunk(far_stress_chunk)
    finish_az(1)
    finish_halos(1)

    receive_halos(2, stress_dz)

    def second_velocity(e):
        velocity_chunk(1, e)
        start_az(4, e)

        @pl.when(e == 0)
        def _():
            send_down(3, vel_dz)

    each_chunk(second_velocity)
    send_up(3, vel_dz)
    for i, (ref, k) in enumerate(vel_place):
        to_out(ref.at[k, inner], vel_out.at[i])
    receive_far_halos(2, far_s)
    each_chunk(far_velocity_chunk)
    finish_az(2)
    finish_az(3)
    finish_halos(2)

    receive_halos(3, vel_dz)
    each_chunk(lambda e: stress_chunk(1, e))
    for i, (ref, k) in enumerate(stress_place):
        to_out(ref.at[k, inner], str_out.at[i])
    finish_az(4)
    finish_halos(3)
    for copy in stores:
        copy.wait()


FAR_DZ = {1: (1, 2), 2: (2,)}


def on_device(depth_devices, az_devices, velocity, stress, memory, layer_ids, materials, jkd, source_depth):
    depth, azims, radii = velocity.shape[1:]
    chunks = depth // 4
    halves = 2 * STEPS
    others = max(az_devices - 1, 1)
    azim_total = azims * az_devices
    radial_high, radial_low = split_high_low(radial_operator(radii).T)
    radial_k = np.concatenate([radial_high, radial_high, radial_low], axis=0)
    azim_high, azim_low = split_high_low(azimuth_operator(azim_total))
    azim_k = np.concatenate([azim_high, azim_high, azim_low], axis=1)
    expand = np.kron(np.eye(radii // 4), np.ones((1, 4))).astype(jnp.bfloat16)
    inverse_r = (1.0 / radial_positions(radii)).astype(np.float32)[None]
    plane = (azims, radii)
    smem = pl.BlockSpec(memory_space=pltpu.SMEM)
    hbm = pl.BlockSpec(memory_space=pltpu.HBM)
    anywhere = pl.BlockSpec(memory_space=pl.ANY)
    vmem = pl.BlockSpec(memory_space=pltpu.VMEM)
    dma = pltpu.SemaphoreType.DMA
    constants = [expand, radial_k, azim_k, inverse_r]
    small = [materials, jkd, layer_ids] + [jnp.asarray(value) for value in constants]

    def held(*shape):
        return pltpu.VMEM(shape + plane, F32)

    return tuple(pl.pallas_call(
        functools.partial(step_kernel, depth_devices, az_devices),
        out_shape=tuple(jax.ShapeDtypeStruct(x.shape, x.dtype) for x in (velocity, stress, memory)),
        in_specs=[smem] + [hbm] * 10,
        out_specs=(anywhere, anywhere, vmem),
        scratch_shapes=[pltpu.VMEM(value.shape, value.dtype) for value in small] + [
            held(4, depth + 1),
            held(3, depth + 1),
            held(4, depth + 1),
            held(2, depth + 1),
            held(others, 4, depth + 1),
            held(others, 4, depth + 1),
            held(others, 2, depth),
            held(others, 1, depth),
            held(others, 1, depth),
            held(others, 3, depth),
            held(1, depth),
            held(1, depth),
            held(halves, 4),
            held(halves, 4),
            held(2, others, 2),
            held(2, others, 2),
            held(halves, 4),
            held(halves, 4),
            held(4, chunks),
            held(others, 2, chunks),
            pltpu.VMEM((NCOEF, chunks, radii), F32),
            held(4, 4),
            pltpu.VMEM((4, azims, 4 * radii), F32),
            dma((21,)),
            dma((13,)),
            dma((5, others, chunks)),
            dma((5, others, chunks)),
            dma((halves, others + 1)),
            dma((halves, others + 1)),
            dma((halves, others + 1)),
            dma((halves, others + 1)),
        ],
        compiler_params=pltpu.CompilerParams(
            collective_id=0, has_side_effects=True, vmem_limit_bytes=40 * 1024 * 1024
        ),
        cost_estimate=pl.CostEstimate(
            flops=10**9, bytes_accessed=2 * 25 * velocity.size // 6 * 4, transcendentals=0
        ),
        name="biot_steps",
    )(source_depth, *small, velocity, stress, memory))


def solution(mesh):
    return jax.shard_map(
        functools.partial(on_device, mesh.shape["depth"], mesh.shape["az"]),
        mesh=mesh,
        in_specs=(
            P(None, "depth", "az", None),
            P(None, "depth", "az", None),
            P(None, "depth", "az", None),
            P("depth", None),
            P(),
            P(),
            P(),
        ),
        out_specs=(
            P(None, "depth", "az", None),
            P(None, "depth", "az", None),
            P(None, "depth", "az", None),
        ),
        check_vma=False,
    )
```

profile of v0, /device:TPU:0, one launch (start us, length us, event | category | flops | bytes accessed | tf_op | source)
XLA Modules:
  0.0 90.1 jit_solution(7758469493912340509)
XLA Ops:
  1.3 0.0 copy-start
  1.3 1.9 %copy-done = f32[12,16,32,128]{3,2,1,0:T(8,128)S(1)} copy-done((f32[12,16,32,128]{3,2,1,0:T(8,128)S(1)}, f32[12,16,32,128]{3,2,1,0:T(8,128)}, u32[]{:S(2)}) %copy-start) | copy-done | bytes 3145752
  3.2 0.0 copy-start.1
  3.2 1.5 %copy-done.1 = f32[7,16,32,128]{3,2,1,0:T(8,128)S(1)} copy-done((f32[7,16,32,128]{3,2,1,0:T(8,128)S(1)}, f32[7,16,32,128]{3,2,1,0:T(8,128)}, u32[]{:S(2)}) %copy-start.1) | copy-done | bytes 1835032
  4.7 0.0 copy-start.2
  4.7 1.4 %copy-done.2 = f32[6,16,32,128]{3,2,1,0:T(8,128)S(1)} copy-done((f32[6,16,32,128]{3,2,1,0:T(8,128)S(1)}, f32[6,16,32,128]{3,2,1,0:T(8,128)}, u32[]{:S(2)}) %copy-start.2) | copy-done | bytes 1572888
  6.1 0.0 copy-start.3
  6.1 0.9 copy-done.3
  7.0 0.0 copy-start.4
  7.0 0.8 copy-done.4
  7.7 0.0 copy-start.5
  7.7 0.7 copy-done.5
  8.4 0.0 copy-start.6
  8.4 0.7 copy-done.6
  9.1 0.0 copy-start.7
  9.1 0.7 copy-done.7
  9.8 0.0 copy-start.8
  9.8 0.7 copy-done.8
  10.5 0.0 copy-start.9
  10.5 0.7 copy-done.9
  11.1 74.9 %biot_steps.1 = (f32[6,16,32,128]{3,2,1,0:T(8,128)S(1)}, f32[7,16,32,128]{3,2,1,0:T(8,128)S(1)}, f32[12,16,32,128]{3,2,1,0:T(8,128)S(1)}) custom-call(s32[1]{0:T(128)S(6)} %copy.17.source, f32[8,8]{1,0:T(8,128)S(1)} %copy-done.6, f32[8,9]{1,0:T(8,128)S(1)} %copy-done.7, s32[4,32]{1,0:T(4,128)S(1)} %copy-done.8, bf16[32,128]{1,0:T(8,128)(2,1)S(1)} %copy-done.5, ...), custom_call_target="tpu_custom_call" | custom-call | flops 1000000000 | bytes 13107200 | tf_op jit(solution)/shard_map/biot_steps/pallas_call | solution.py:627
  86.1 1.1 %copy.18 = f32[6,16,32,128]{3,2,1,0:T(8,128)} copy(f32[6,16,32,128]{3,2,1,0:T(8,128)S(1)} %get-tuple-element.6) | data formatting | bytes 3145728
  87.2 1.2 %copy.19 = f32[7,16,32,128]{3,2,1,0:T(8,128)} copy(f32[7,16,32,128]{3,2,1,0:T(8,128)S(1)} %get-tuple-element.7) | data formatting | bytes 3670016
  88.4 1.7 %copy.20 = f32[12,16,32,128]{3,2,1,0:T(8,128)} copy(f32[12,16,32,128]{3,2,1,0:T(8,128)S(1)} %get-tuple-element.8) | data formatting | bytes 6291456
Async XLA Ops:
  1.3 1.9 %copy-start = (f32[12,16,32,128]{3,2,1,0:T(8,128)S(1)}, f32[12,16,32,128]{3,2,1,0:T(8,128)}, u32[]{:S(2)}) copy-start(f32[12,16,32,128]{3,2,1,0:T(8,128)} %mem_in.1) | copy-start | bytes 9437188
  3.2 1.5 %copy-start.1 = (f32[7,16,32,128]{3,2,1,0:T(8,128)S(1)}, f32[7,16,32,128]{3,2,1,0:T(8,128)}, u32[]{:S(2)}) copy-start(f32[7,16,32,128]{3,2,1,0:T(8,128)} %str_in.1) | copy-start | bytes 5505028
  4.7 1.4 %copy-start.2 = (f32[6,16,32,128]{3,2,1,0:T(8,128)S(1)}, f32[6,16,32,128]{3,2,1,0:T(8,128)}, u32[]{:S(2)}) copy-start(f32[6,16,32,128]{3,2,1,0:T(8,128)} %vel_in.1) | copy-start | bytes 4718596
  6.1 0.9 copy-start.3
  7.0 0.8 copy-start.4
  7.7 0.7 copy-start.5
  8.4 0.7 copy-start.6
  9.1 0.7 copy-start.7
  9.8 0.7 copy-start.8
  10.5 0.7 copy-start.9
where the time goes:
time: 91.3 us; the launch traced here: 90.1 us
  Pallas kernels  74.9 us (82%)
  local copies, waits for them, and re-layouts  13.9 us (15%)
  between operations  1.31 us (1%)
    pallas_call x1, Pallas kernels, on_device(): pl.pallas_call(functools.partial(step_kernel, depth_devices, az_devices),...  74.9 us
    unnamed x23, local copies, waits for them, and re-layouts  13.9 us

commit v1 on v0

--- a/solution.py
+++ b/solution.py
@@ -45,12 +45,6 @@
     return (assembled / node_mass[:, None])[:node_count, :node_count]
 
 
-def radial_positions(node_count):
-    gll_nodes, weights, derivative = gll_basis()
-    positions = np.arange(node_count)
-    return R_INNER + positions // 4 + 0.5 * (1.0 + gll_nodes[positions % 4])
-
-
 def azimuth_operator(node_count):
     positions = np.arange(node_count)
     offsets = positions[:, None] - positions[None, :]
@@ -81,13 +75,13 @@
 
 def step_kernel(
     depth_devices, az_devices,
-    source, mats_in, jkd_in, ids_in, expand_in, radial_in, azim_in, inv_r_in, vel_in, str_in, mem_in,
-    vel_out, str_out, mem,
-    mats, jkd, ids, expand, radial_k, azim_k, inv_r,
-    s_az, s_rest, v_az, v_rest, far_s, far_v, far_new, far_dw, far_psi, far_dt, dw, psi_t,
+    source, mats_in, jkd_in, ids_in, radial_in, azim_in, vel_in, str_in, mem_in,
+    vel_out, str_out, mem_out,
+    mats, jkd, ids, radial_k, azim_k,
+    mem, inv_r, s_az, s_rest, v_az, v_rest, far_s, far_v, far_new, far_dw, far_psi, far_dt, dw, psi_t,
     halo_above, halo_below, far_above, far_below, up_stage, down_stage,
     partial, far_partial, coef, rad_d, az_d,
-    load_sem, store_sem, az_send, az_recv, up_send, up_recv, down_send, down_recv,
+    load_sem, store_sem, chunk_sem, az_send, az_recv, up_send, up_recv, down_send, down_recv,
 ):
     me_d = lax.axis_index("depth")
     me_a = lax.axis_index("az")
@@ -96,7 +90,7 @@
     others = range(az_devices - 1)
     has_up = me_d < depth_devices - 1
     has_down = me_d > 0
-    _, weights, derivative = gll_basis()
+    gll_nodes, weights, derivative = gll_basis()
     stencil = weights[:, None] * derivative * 2.0
 
     inner = pl.ds(0, depth)
@@ -104,12 +98,12 @@
     vel_place = [(v_az, 0), (v_az, 2), (v_az, 1), (v_rest, 0), (v_az, 3), (v_rest, 1)]
     pairs = [(str_in.at[i], ref.at[k, inner]) for i, (ref, k) in enumerate(stress_place)]
     pairs += [(vel_in.at[i], ref.at[k, inner]) for i, (ref, k) in enumerate(vel_place)]
-    pairs += [(mem_in, mem), (mats_in, mats), (jkd_in, jkd), (ids_in, ids), (expand_in, expand)]
-    pairs += [(radial_in, radial_k), (azim_in, azim_k), (inv_r_in, inv_r)]
+    pairs += [(mem_in, mem), (mats_in, mats), (jkd_in, jkd), (ids_in, ids)]
+    pairs += [(radial_in, radial_k), (azim_in, azim_k)]
     loads = [
         pltpu.make_async_copy(src, dst, load_sem.at[i]) for i, (src, dst) in enumerate(pairs)
     ]
-    for index in (1, 3, 5, 6, 14, 15, 16, 17, 0, 2, 4, 18, 19, 20, 7, 8, 9, 10, 11, 12, 13):
+    for index in (1, 3, 5, 6, 14, 15, 16, 0, 2, 4, 17, 18, 7, 8, 9, 10, 11, 12, 13):
         loads[index].start()
 
     def other_az(k, sign):
@@ -251,35 +245,37 @@
             for f, (ref, k) in enumerate(dz_fields):
                 partial[f, 0] = bottom_of(reader(ref, k))
 
-    def receive_far_halos(half, ref):
-        first, count = far_fields[half]
-        fields = [(k, i, FAR_DZ[half][i]) for k in others for i in range(count)]
-        for e in range(1, chunks):
-            for k, i, f in fields:
-                far_partial[k, i, e] = top_of(far_reader(ref, k, f), 4 * (e - 1))
-
+    def far_list(half):
+        return [(k, i, f) for k in others for i, f in enumerate(FAR_DZ[half])]
+
+    def far_partials(half, ref, e):
+        for k, i, f in far_list(half):
+            far_partial[k, i, e] = top_of(far_reader(ref, k, f), 4 * (e - 1))
+
+    def receive_far_top(half, ref):
         @pl.when(has_up)
         def _():
             for copy in down_copies(half)[1:]:
                 copy.wait_recv()
-            for k, i, f in fields:
+            for k, i, f in far_list(half):
                 ref[k, f, depth] = far_above[half - 1, k, i]
 
         @pl.when(jnp.logical_not(has_up))
         def _():
-            for k, i, f in fields:
+            for k, i, f in far_list(half):
                 ref[k, f, depth] = jnp.zeros((azims, radii), F32)
 
+    def receive_far_bottom(half, ref):
         @pl.when(has_down)
         def _():
             for copy in up_copies(half)[1:]:
                 copy.wait_recv()
-            for k, i, f in fields:
+            for k, i, f in far_list(half):
                 far_partial[k, i, 0] = far_below[half - 1, k, i]
 
         @pl.when(jnp.logical_not(has_down))
         def _():
-            for k, i, f in fields:
+            for k, i, f in far_list(half):
                 far_partial[k, i, 0] = bottom_of(far_reader(ref, k, f))
 
     def finish_az(which):
@@ -488,18 +484,30 @@
 
     for index in (1, 3, 5, 6):
         loads[index].wait()
-    for e in range(chunks):
+    order = [0] + ([chunks - 1] if chunks > 1 else []) + list(range(1, chunks - 1))
+    for e in order:
         start_az(0, e)
     for index in (0, 2, 4):
         loads[index].wait()
     send_down(0, stress_dz)
     send_up(0, stress_dz)
-    for index in range(14, 21):
+    for index in range(14, 19):
         loads[index].wait()
 
+    elements = ids.shape[1]
+    spread = lax.broadcasted_iota(jnp.int32, (elements, radii), 0) == (
+        lax.broadcasted_iota(jnp.int32, (elements, radii), 1) >> 2
+    )
     ids_node = jnp.dot(
-        ids[...].astype(F32).astype(BF16), expand[...], preferred_element_type=F32
+        ids[...].astype(F32).astype(BF16), spread.astype(F32).astype(BF16),
+        preferred_element_type=F32,
     )
+    node = lax.broadcasted_iota(jnp.int32, (1, radii), 1)
+    place = node & 3
+    inside = jnp.zeros((1, radii), F32)
+    for j in range(1, 4):
+        inside = jnp.where(place == j, np.float32(0.5 * (1.0 + gll_nodes[j])), inside)
+    inv_r[...] = 1.0 / (np.float32(R_INNER) + (node >> 2).astype(F32) + inside)
 
     def pick(table, column):
         value = jnp.zeros_like(ids_node)
@@ -535,16 +543,28 @@
 
     receive_halos(0, stress_dz)
 
-    def first_velocity(e):
+    def first_velocity(turn):
+        last = chunks - 1
+        e = jnp.where(turn == 0, 0, jnp.where(turn == 1, last, turn - 1))
         velocity_chunk(0, e)
-        start_az(1, e)
-
-        @pl.when(e == 0)
+
+        @pl.when(turn == 0)
         def _():
             send_down(1, vel_dz)
 
+        @pl.when(turn == min(1, last))
+        def _():
+            send_up(1, vel_dz)
+
+        @pl.when((turn != 1) | (last == 1))
+        def _():
+            start_az(1, e)
+
+        @pl.when((turn == last) & (last > 1))
+        def _():
+            start_az(1, last)
+
     each_chunk(first_velocity)
-    send_up(1, vel_dz)
     for e in range(chunks):
         start_az(2, e)
     finish_az(0)
@@ -560,10 +580,22 @@
         def _():
             send_down(2, stress_dz)
 
+        @pl.when(e == chunks - 1)
+        def _():
+            send_up(2, stress_dz)
+            receive_far_top(1, far_v)
+
+        @pl.when(e == 1)
+        def _():
+            receive_far_bottom(1, far_v)
+
+        @pl.when(e > 0)
+        def _():
+            far_partials(1, far_v, e)
+            far_stress_chunk(e - 1)
+
     each_chunk(first_stress)
-    send_up(2, stress_dz)
-    receive_far_halos(1, far_v)
-    each_chunk(far_stress_chunk)
+    far_stress_chunk(chunks - 1)
     finish_az(1)
     finish_halos(1)
 
@@ -581,20 +613,38 @@
     send_up(3, vel_dz)
     for i, (ref, k) in enumerate(vel_place):
         to_out(ref.at[k, inner], vel_out.at[i])
-    receive_far_halos(2, far_s)
+    to_out(mem, mem_out)
+    receive_far_top(2, far_s)
+    receive_far_bottom(2, far_s)
+    for e in range(1, chunks):
+        far_partials(2, far_s, e)
     each_chunk(far_velocity_chunk)
     finish_az(2)
     finish_az(3)
     finish_halos(2)
 
     receive_halos(3, vel_dz)
-    each_chunk(lambda e: stress_chunk(1, e))
-    for i, (ref, k) in enumerate(stress_place):
-        to_out(ref.at[k, inner], str_out.at[i])
+
+    def chunk_stores(e):
+        planes = pl.ds(pl.multiple_of(4 * e, 4), 4)
+        return [
+            pltpu.make_async_copy(ref.at[k, planes], str_out.at[i, planes], chunk_sem.at[e, i])
+            for i, (ref, k) in enumerate(stress_place)
+        ]
+
+    def second_stress(e):
+        stress_chunk(1, e)
+        for copy in chunk_stores(e):
+            copy.start()
+
+    each_chunk(second_stress)
     finish_az(4)
     finish_halos(3)
     for copy in stores:
         copy.wait()
+    for e in range(chunks):
+        for copy in chunk_stores(e):
+            copy.wait()
 
 
 FAR_DZ = {1: (1, 2), 2: (2,)}
@@ -610,15 +660,11 @@
     radial_k = np.concatenate([radial_high, radial_high, radial_low], axis=0)
     azim_high, azim_low = split_high_low(azimuth_operator(azim_total))
     azim_k = np.concatenate([azim_high, azim_high, azim_low], axis=1)
-    expand = np.kron(np.eye(radii // 4), np.ones((1, 4))).astype(jnp.bfloat16)
-    inverse_r = (1.0 / radial_positions(radii)).astype(np.float32)[None]
     plane = (azims, radii)
     smem = pl.BlockSpec(memory_space=pltpu.SMEM)
     hbm = pl.BlockSpec(memory_space=pltpu.HBM)
-    anywhere = pl.BlockSpec(memory_space=pl.ANY)
-    vmem = pl.BlockSpec(memory_space=pltpu.VMEM)
     dma = pltpu.SemaphoreType.DMA
-    constants = [expand, radial_k, azim_k, inverse_r]
+    constants = [radial_k, azim_k]
     small = [materials, jkd, layer_ids] + [jnp.asarray(value) for value in constants]
 
     def held(*shape):
@@ -627,9 +673,11 @@
     return tuple(pl.pallas_call(
         functools.partial(step_kernel, depth_devices, az_devices),
         out_shape=tuple(jax.ShapeDtypeStruct(x.shape, x.dtype) for x in (velocity, stress, memory)),
-        in_specs=[smem] + [hbm] * 10,
-        out_specs=(anywhere, anywhere, vmem),
+        in_specs=[smem] + [hbm] * 8,
+        out_specs=(hbm, hbm, hbm),
         scratch_shapes=[pltpu.VMEM(value.shape, value.dtype) for value in small] + [
+            held(12, depth),
+            pltpu.VMEM((1, radii), F32),
             held(4, depth + 1),
             held(3, depth + 1),
             held(4, depth + 1),
@@ -653,8 +701,9 @@
             pltpu.VMEM((NCOEF, chunks, radii), F32),
             held(4, 4),
             pltpu.VMEM((4, azims, 4 * radii), F32),
-            dma((21,)),
-            dma((13,)),
+            dma((19,)),
+            dma((7,)),
+            dma((chunks, 7)),
             dma((5, others, chunks)),
             dma((5, others, chunks)),
             dma((halves, others + 1)),
@@ -663,7 +712,7 @@
             dma((halves, others + 1)),
         ],
         compiler_params=pltpu.CompilerParams(
-            collective_id=0, has_side_effects=True, vmem_limit_bytes=40 * 1024 * 1024
+            collective_id=0, has_side_effects=True, vmem_limit_bytes=64 * 1024 * 1024
         ),
         cost_estimate=pl.CostEstimate(
             flops=10**9, bytes_accessed=2 * 25 * velocity.size // 6 * 4, transcendentals=0

time: 91.3 us -> 85.3 us (0.934); the launches traced: 90.1 us -> 85.1 us
  local copies, waits for them, and re-layouts: 13.9 us -> 7.11 us
  Pallas kernels: 74.9 us -> 76.7 us
    unnamed x23 -> x7, local copies, waits for them, and re-layouts: 13.9 us -> 7.11 us
    pallas_call x1, Pallas kernels: 74.9 us -> 76.7 us  [on_device(): pl.pallas_call(functools.partial(step_kernel, depth_devices, az_devices),...]
where the time goes in v1:
time: 85.3 us; the launch traced here: 85.1 us
  Pallas kernels  76.7 us (90%)
  local copies, waits for them, and re-layouts  7.11 us (8%)
  between operations  1.3 us (2%)
    pallas_call x1, Pallas kernels, on_device(): pl.pallas_call(functools.partial(step_kernel, depth_devices, az_devices),...  76.7 us
    unnamed x7, local copies, waits for them, and re-layouts  7.11 us

profile of v1, /device:TPU:0, one launch (start us, length us, event | category | flops | bytes accessed | tf_op | source)
XLA Modules:
  0.0 85.1 jit_solution(16805561068547048641)
XLA Ops:
  1.3 76.7 %biot_steps.1 = (f32[6,16,32,128]{3,2,1,0:T(8,128)}, f32[7,16,32,128]{3,2,1,0:T(8,128)}, f32[12,16,32,128]{3,2,1,0:T(8,128)}) custom-call(s32[1]{0:T(128)S(6)} %copy.15.source, f32[8,8]{1,0:T(8,128)} %mats_in.1, f32[8,9]{1,0:T(8,128)} %jkd_in.1, s32[4,32]{1,0:T(4,128)} %ids_in.1, bf16[384,128]{1,0:T(8,128)(2,1)} %constant.4.clone.radial_in, ...), custom_call_target="tpu_custom_call" | custom-call | flops 1000000000 | bytes 13107200 | tf_op jit(solution)/shard_map/biot_steps/pallas_call | solution.py:673
  78.0 0.0 copy-start.1
  78.0 2.9 %copy.16 = f32[6,16,32,128]{3,2,1,0:T(8,128)} copy(f32[6,16,32,128]{3,2,1,0:T(8,128)} %get-tuple-element.6) | data formatting | bytes 3145728
  80.9 0.0 copy-done.1
  80.9 0.0 copy-start
  80.9 1.2 %copy.17 = f32[7,16,32,128]{3,2,1,0:T(8,128)} copy(f32[7,16,32,128]{3,2,1,0:T(8,128)S(1)} %copy-done.1) | data formatting | bytes 3670016
  82.1 1.3 %copy-done = f32[12,16,32,128]{3,2,1,0:T(8,128)S(1)} copy-done((f32[12,16,32,128]{3,2,1,0:T(8,128)S(1)}, f32[12,16,32,128]{3,2,1,0:T(8,128)}, u32[]{:S(2)}) %copy-start) | copy-done | bytes 3145752
  83.4 1.7 %copy.18 = f32[12,16,32,128]{3,2,1,0:T(8,128)} copy(f32[12,16,32,128]{3,2,1,0:T(8,128)S(1)} %copy-done) | data formatting | bytes 6291456
Async XLA Ops:
  78.0 2.9 %copy-start.1 = (f32[7,16,32,128]{3,2,1,0:T(8,128)S(1)}, f32[7,16,32,128]{3,2,1,0:T(8,128)}, u32[]{:S(2)}) copy-start(f32[7,16,32,128]{3,2,1,0:T(8,128)} %get-tuple-element.7) | copy-start | bytes 5505028
  80.9 2.6 %copy-start = (f32[12,16,32,128]{3,2,1,0:T(8,128)S(1)}, f32[12,16,32,128]{3,2,1,0:T(8,128)}, u32[]{:S(2)}) copy-start(f32[12,16,32,128]{3,2,1,0:T(8,128)} %get-tuple-element.8) | copy-start | bytes 9437188

commit v2 on v1

--- a/solution.py
+++ b/solution.py
@@ -76,12 +76,12 @@
 def step_kernel(
     depth_devices, az_devices,
     source, mats_in, jkd_in, ids_in, radial_in, azim_in, vel_in, str_in, mem_in,
-    vel_out, str_out, mem_out,
+    coef_out, inv_r_out, partial_out, sa_out, sr_out, va_out, vr_out, fv_out, far_new, mem_out,
     mats, jkd, ids, radial_k, azim_k,
-    mem, inv_r, s_az, s_rest, v_az, v_rest, far_s, far_v, far_new, far_dw, far_psi, far_dt, dw, psi_t,
+    mem, inv_r, s_az, s_rest, v_az, v_rest, far_s, far_v, far_dw, far_psi, far_dt, dw, psi_t,
     halo_above, halo_below, far_above, far_below, up_stage, down_stage,
     partial, far_partial, coef, rad_d, az_d,
-    load_sem, store_sem, chunk_sem, az_send, az_recv, up_send, up_recv, down_send, down_recv,
+    load_sem, first_sem, store_sem, az_send, az_recv, up_send, up_recv, down_send, down_recv,
 ):
     me_d = lax.axis_index("depth")
     me_a = lax.axis_index("az")
@@ -103,7 +103,21 @@
     loads = [
         pltpu.make_async_copy(src, dst, load_sem.at[i]) for i, (src, dst) in enumerate(pairs)
     ]
-    for index in (1, 3, 5, 6, 14, 15, 16, 0, 2, 4, 17, 18, 7, 8, 9, 10, 11, 12, 13):
+    order = [0] + ([chunks - 1] if chunks > 1 else []) + list(range(1, chunks - 1))
+
+    def first_loads(e):
+        planes = pl.ds(4 * e, 4)
+        return [
+            pltpu.make_async_copy(
+                str_in.at[i, planes], s_az.at[k, planes], first_sem.at[e, k]
+            )
+            for k, i in enumerate((3, 1, 5, 6))
+        ]
+
+    for e in order:
+        for copy in first_loads(e):
+            copy.start()
+    for index in (14, 15, 16, 0, 2, 4, 17, 18, 7, 8, 9, 10, 11, 12, 13):
         loads[index].start()
 
     def other_az(k, sign):
@@ -402,13 +416,9 @@
         base = pl.multiple_of(4 * e, 4)
         planes = pl.ds(base, 4)
         radial_part([v_az[0, planes], v_az[2, planes], v_az[1, planes], v_rest[0, planes]])
-        if step == 0:
-            receive_az(1, e)
-            far = [(far_v, f) for f in range(4)]
-        else:
-            receive_az(4, e)
-            far = [(far_new, 0), (far_new, 1), (far_v, 2), (far_v, 3)]
-        azimuth_part([(v_az, f) for f in range(4)], far, base, (0, 1, 2) if step == 0 else ())
+        receive_az(1, e)
+        far = [(far_v, f) for f in range(4)]
+        azimuth_part([(v_az, f) for f in range(4)], far, base, (0, 1, 2))
         row = row_of(e)
         q = inv_r[...]
         for j in range(4):
@@ -482,10 +492,9 @@
 
         lax.fori_loop(0, chunks, wrapped, 0)
 
-    for index in (1, 3, 5, 6):
-        loads[index].wait()
-    order = [0] + ([chunks - 1] if chunks > 1 else []) + list(range(1, chunks - 1))
     for e in order:
+        for copy in first_loads(e):
+            copy.wait()
         start_az(0, e)
     for index in (0, 2, 4):
         loads[index].wait()
@@ -600,6 +609,10 @@
     finish_halos(1)
 
     receive_halos(2, stress_dz)
+    to_out(s_az.at[:, inner], sa_out)
+    to_out(s_rest.at[:, inner], sr_out)
+    to_out(coef, coef_out)
+    to_out(inv_r, inv_r_out)
 
     def second_velocity(e):
         velocity_chunk(1, e)
@@ -611,19 +624,158 @@
 
     each_chunk(second_velocity)
     send_up(3, vel_dz)
-    for i, (ref, k) in enumerate(vel_place):
-        to_out(ref.at[k, inner], vel_out.at[i])
+    to_out(v_az.at[:, inner], va_out.at[:, inner])
+    to_out(v_rest.at[:, inner], vr_out.at[:, inner])
     to_out(mem, mem_out)
     receive_far_top(2, far_s)
     receive_far_bottom(2, far_s)
     for e in range(1, chunks):
         far_partials(2, far_s, e)
     each_chunk(far_velocity_chunk)
+    to_out(far_v.at[:, pl.ds(2, 2), inner], fv_out)
+    receive_halos(3, vel_dz)
+    edge = pl.ds(depth, 1)
+    to_out(v_az.at[pl.ds(0, 3), edge], va_out.at[pl.ds(0, 3), edge])
+    to_out(v_rest.at[pl.ds(1, 1), edge], vr_out.at[pl.ds(1, 1), edge])
+    to_out(partial, partial_out)
     finish_az(2)
     finish_az(3)
     finish_halos(2)
-
-    receive_halos(3, vel_dz)
+    for e in range(chunks):
+        receive_az(4, e)
+    finish_az(4)
+    finish_halos(3)
+    for copy in stores:
+        copy.wait()
+
+
+FAR_DZ = {1: (1, 2), 2: (2,)}
+
+
+def finish_kernel(
+    az_devices,
+    source, radial_in, azim_in, coef_in, inv_r_in, partial_in, sa_in, sr_in, va_in, vr_in, fv_in,
+    fn_in, mem_in,
+    vel_out, str_out, mem_out,
+    radial_k, azim_k, coef, inv_r, partial, s_az, s_rest, v_az, v_rest, far_v, far_new,
+    rad_d, az_d,
+    load_sem, load_chunk_sem, move_sem, chunk_sem,
+):
+    me_d = lax.axis_index("depth")
+    depth, azims, radii = s_az.shape[1:]
+    chunks = depth // 4
+    others = range(az_devices - 1)
+    gll_nodes, weights, derivative = gll_basis()
+    stencil = weights[:, None] * derivative * 2.0
+
+    def reader(ref, k):
+        return lambda z: ref[k, z]
+
+    def dz_at(read, below, base, j):
+        if j == 0:
+            total = weighted([(stencil[0, l], read(base + l)) for l in range(1, 5)])
+            return (total + below) * np.float32(1.0 / (2.0 * weights[0]))
+        return weighted([(2.0 * derivative[j, l], read(base + l)) for l in range(5)])
+
+    def high_low(value, axis):
+        high = value.astype(BF16)
+        low = (value - high.astype(F32)).astype(BF16)
+        return jnp.concatenate([high, low, high], axis=axis)
+
+    def radial_part(blocks):
+        rows = jnp.concatenate([block.reshape(4 * azims, radii) for block in blocks], axis=0)
+        result = jnp.dot(high_low(rows, 1), radial_k[...], preferred_element_type=F32)
+        rad_d[0 : len(blocks)] = result.reshape(len(blocks), 4, azims, radii)
+
+    def azimuth_part(near, far, base):
+        rows = azims
+        for j in range(4):
+            blocks = [jnp.concatenate([ref[f, base + j] for ref, f in near], axis=1)]
+            for k in others:
+                blocks.append(jnp.concatenate([ref[k, f, base + j] for ref, f in far], axis=1))
+            column = jnp.concatenate(blocks, axis=0)
+            result = jnp.dot(
+                azim_k[0:rows, :], high_low(column, 0), preferred_element_type=F32
+            )
+            az_d[j] = result[0:azims]
+
+    def az_at(j, f):
+        return az_d[j, :, f * radii : (f + 1) * radii]
+
+    def row_of(e):
+        def row(index):
+            return coef[index, pl.ds(e, 1), :]
+
+        return row
+
+    def shot_at(step, z):
+        gain = np.float32(DT * SOURCE_GAIN * math.cos(0.9 * step))
+        lane = lax.broadcasted_iota(jnp.int32, (1, radii), 1)
+        wanted = jnp.zeros((1, radii), jnp.int32) + source[0]
+        return jnp.where((wanted == me_d * depth + z) & (lane < 4 * RB), gain, np.float32(0.0))
+
+    def stress_chunk(step, e):
+        base = pl.multiple_of(4 * e, 4)
+        planes = pl.ds(base, 4)
+        radial_part([v_az[0, planes], v_az[2, planes], v_az[1, planes], v_rest[0, planes]])
+        far = [(far_new, 0), (far_new, 1), (far_v, 0), (far_v, 1)]
+        azimuth_part([(v_az, f) for f in range(4)], far, base)
+        row = row_of(e)
+        q = inv_r[...]
+        for j in range(4):
+            z = base + j
+            vr, vt, wr = v_az[0, z], v_az[2, z], v_rest[0, z]
+            dz = [
+                dz_at(reader(ref, k), partial[f, e], base, j)
+                for f, (ref, k) in enumerate(vel_dz)
+            ]
+            e_rr = rad_d[0, j]
+            e_tt = q * (vr + az_at(j, 2))
+            e_zz = dz[1]
+            g_rt = q * (az_at(j, 0) - vt) + rad_d[1, j]
+            g_rz = dz[0] + rad_d[2, j]
+            g_tz = dz[2] + q * az_at(j, 1)
+            div_v = e_rr + e_tt + e_zz
+            div_w = rad_d[3, j] + q * (wr + az_at(j, 3)) + dz[3]
+            bulk = row(LF) * div_v + row(BM) * div_w
+            twice = 2.0 * row(MU)
+            s_rest[0, z] = s_rest[0, z] + (bulk + twice * e_rr)
+            s_az[1, z] = s_az[1, z] + (bulk + twice * e_tt)
+            s_rest[1, z] = s_rest[1, z] + (bulk + twice * e_zz)
+            s_az[0, z] = s_az[0, z] + row(MU) * g_rt
+            s_rest[2, z] = s_rest[2, z] + row(MU) * g_rz
+            s_az[2, z] = s_az[2, z] + row(MU) * g_tz
+            s_az[3, z] = s_az[3, z] - (row(BM) * div_v + row(PM) * div_w) + shot_at(step, z)
+
+    vel_dz = [(v_az, 0), (v_az, 1), (v_az, 2), (v_rest, 1)]
+
+    def chunk_loads(e):
+        planes = pl.ds(pl.multiple_of(4 * e, 4), 4)
+        pairs = [(ref_in.at[:, planes], ref.at[:, planes]) for ref_in, ref in ((sa_in, s_az), (sr_in, s_rest))]
+        pairs += [
+            (ref_in.at[:, :, planes], ref.at[:, :, planes])
+            for ref_in, ref in ((fv_in, far_v), (fn_in, far_new))
+        ]
+        return [
+            pltpu.make_async_copy(src, dst, load_chunk_sem.at[e, i])
+            for i, (src, dst) in enumerate(pairs)
+        ]
+
+    pairs = [(va_in, v_az), (vr_in, v_rest), (partial_in, partial), (radial_in, radial_k)]
+    pairs += [(azim_in, azim_k), (coef_in, coef), (inv_r_in, inv_r)]
+    loads = [pltpu.make_async_copy(src, dst, load_sem.at[i]) for i, (src, dst) in enumerate(pairs)]
+    for copy in loads:
+        copy.start()
+    for e in range(chunks):
+        for copy in chunk_loads(e):
+            copy.start()
+    for copy in loads:
+        copy.wait()
+    vel_place = [(v_az, 0), (v_az, 2), (v_az, 1), (v_rest, 0), (v_az, 3), (v_rest, 1)]
+    stress_place = [(s_rest, 0), (s_az, 1), (s_rest, 1), (s_az, 0), (s_rest, 2), (s_az, 2), (s_az, 3)]
+    moves = [(mem_in, mem_out)]
+    moves += [(ref.at[k, pl.ds(0, depth)], vel_out.at[i]) for i, (ref, k) in enumerate(vel_place)]
+    moves = [pltpu.make_async_copy(src, dst, move_sem.at[i]) for i, (src, dst) in enumerate(moves)]
 
     def chunk_stores(e):
         planes = pl.ds(pl.multiple_of(4 * e, 4), 4)
@@ -632,22 +784,26 @@
             for i, (ref, k) in enumerate(stress_place)
         ]
 
-    def second_stress(e):
-        stress_chunk(1, e)
+    def body(e, carry):
+        for copy in chunk_loads(e):
+            copy.wait()
+
+        @pl.when(e == 0)
+        def _():
+            for copy in moves:
+                copy.start()
+
+        stress_chunk(STEPS - 1, e)
         for copy in chunk_stores(e):
             copy.start()
-
-    each_chunk(second_stress)
-    finish_az(4)
-    finish_halos(3)
-    for copy in stores:
+        return carry
+
+    lax.fori_loop(0, chunks, body, 0)
+    for copy in moves:
         copy.wait()
     for e in range(chunks):
         for copy in chunk_stores(e):
             copy.wait()
-
-
-FAR_DZ = {1: (1, 2), 2: (2,)}
 
 
 def on_device(depth_devices, az_devices, velocity, stress, memory, layer_ids, materials, jkd, source_depth):
@@ -670,11 +826,26 @@
     def held(*shape):
         return pltpu.VMEM(shape + plane, F32)
 
-    return tuple(pl.pallas_call(
+    def whole(*shape):
+        return jax.ShapeDtypeStruct(shape + plane, F32)
+
+    coef_shape = (NCOEF, chunks, radii)
+    parts = pl.pallas_call(
         functools.partial(step_kernel, depth_devices, az_devices),
-        out_shape=tuple(jax.ShapeDtypeStruct(x.shape, x.dtype) for x in (velocity, stress, memory)),
+        out_shape=(
+            jax.ShapeDtypeStruct(coef_shape, F32),
+            jax.ShapeDtypeStruct((1, radii), F32),
+            whole(4, chunks),
+            whole(4, depth),
+            whole(3, depth),
+            whole(4, depth + 1),
+            whole(2, depth + 1),
+            whole(others, 2, depth),
+            whole(others, 2, depth),
+            whole(12, depth),
+        ),
         in_specs=[smem] + [hbm] * 8,
-        out_specs=(hbm, hbm, hbm),
+        out_specs=(hbm,) * 10,
         scratch_shapes=[pltpu.VMEM(value.shape, value.dtype) for value in small] + [
             held(12, depth),
             pltpu.VMEM((1, radii), F32),
@@ -684,7 +855,6 @@
             held(2, depth + 1),
             held(others, 4, depth + 1),
             held(others, 4, depth + 1),
-            held(others, 2, depth),
             held(others, 1, depth),
             held(others, 1, depth),
             held(others, 3, depth),
@@ -698,12 +868,12 @@
             held(halves, 4),
             held(4, chunks),
             held(others, 2, chunks),
-            pltpu.VMEM((NCOEF, chunks, radii), F32),
+            pltpu.VMEM(coef_shape, F32),
             held(4, 4),
             pltpu.VMEM((4, azims, 4 * radii), F32),
             dma((19,)),
-            dma((7,)),
-            dma((chunks, 7)),
+            dma((chunks, 4)),
+            dma((11,)),
             dma((5, others, chunks)),
             dma((5, others, chunks)),
             dma((halves, others + 1)),
@@ -718,7 +888,37 @@
             flops=10**9, bytes_accessed=2 * 25 * velocity.size // 6 * 4, transcendentals=0
         ),
         name="biot_steps",
-    )(source_depth, *small, velocity, stress, memory))
+    )(source_depth, *small, velocity, stress, memory)
+    return tuple(pl.pallas_call(
+        functools.partial(finish_kernel, az_devices),
+        out_shape=tuple(jax.ShapeDtypeStruct(x.shape, x.dtype) for x in (velocity, stress, memory)),
+        in_specs=[smem] + [hbm] * 12,
+        out_specs=(hbm,) * 3,
+        scratch_shapes=[
+            pltpu.VMEM(radial_k.shape, BF16),
+            pltpu.VMEM(azim_k.shape, BF16),
+            pltpu.VMEM(coef_shape, F32),
+            pltpu.VMEM((1, radii), F32),
+            held(4, chunks),
+            held(4, depth),
+            held(3, depth),
+            held(4, depth + 1),
+            held(2, depth + 1),
+            held(others, 2, depth),
+            held(others, 2, depth),
+            held(4, 4),
+            pltpu.VMEM((4, azims, 4 * radii), F32),
+            dma((7,)),
+            dma((chunks, 4)),
+            dma((7,)),
+            dma((chunks, 7)),
+        ],
+        compiler_params=pltpu.CompilerParams(vmem_limit_bytes=64 * 1024 * 1024),
+        cost_estimate=pl.CostEstimate(
+            flops=10**9, bytes_accessed=2 * 25 * velocity.size // 6 * 4, transcendentals=0
+        ),
+        name="biot_finish",
+    )(source_depth, *small[3:], *parts))
 
 
 def solution(mesh):

time: 85.3 us -> 176 us (2.06)
  Pallas kernels: 76.7 us -> 175 us
  local copies, waits for them, and re-layouts: 7.11 us -> 0 us
    pallas_call x0 -> x1, Pallas kernels: none -> 99.2 us  [on_device(): pl.pallas_call(functools.partial(finish_kernel, az_devices), out_shape=tu...]
    unnamed x7 -> x0, local copies, waits for them, and re-layouts: 7.11 us -> none
where the time goes in v2:
time: 176 us
  Pallas kernels  175 us (99%)
    pallas_call x1, Pallas kernels, on_device(): pl.pallas_call(functools.partial(finish_kernel, az_devices), out_shape=tu...  99.2 us
    pallas_call x1, Pallas kernels, on_device(): pl.pallas_call(functools.partial(step_kernel, depth_devices, az_devices),...  75.6 us

profile of v2, /device:TPU:0, one launch (start us, length us, event | category | flops | bytes accessed | tf_op | source)
XLA Modules:
  0.0 176.1 jit_solution(3568497138719295320)
XLA Ops:
  1.3 75.6 %biot_steps.1 = (f32[16,4,128]{2,1,0:T(4,128)}, f32[1,128]{1,0:T(1,128)}, f32[4,4,32,128]{3,2,1,0:T(8,128)}, f32[4,16,32,128]{3,2,1,0:T(8,128)}, f32[3,16,32,128...) custom-call(s32[1]{0:T(128)S(6)} %copy.12.source, ...), custom_call_target="tpu_custom_call" | custom-call | flops 1000000000 | bytes 13107200 | tf_op jit(solution)/shard_map/biot_steps/pallas_call | solution.py:833
  76.9 99.2 %biot_finish.1 = (f32[6,16,32,128]{3,2,1,0:T(8,128)}, f32[7,16,32,128]{3,2,1,0:T(8,128)}, f32[12,16,32,128]{3,2,1,0:T(8,128)}) custom-call(s32[1]{0:T(128)S(6)} %copy.12.source, bf16[384,128]{1,0:T(8,128)(2,1)} %constant.4.clone.radial_in, bf16[64,192]{1,0:T(8,128)(2,1)} %constant.5.clone.azim_in, f32[16,4,128]{2,1,0:T(4,128)} %get-tuple-element.13.coef_in, ...), custom_call_target="tpu_custom_call" | custom-call | flops 1000000000 | bytes 13107200 | tf_op jit(solution)/shard_map/biot_finish/pallas_call | solution.py:892

commit v3 on v1

--- a/solution.py
+++ b/solution.py
@@ -650,6 +650,24 @@
 FAR_DZ = {1: (1, 2), 2: (2,)}
 
 
+def deliver_kernel(vel_in, str_in, mem_in, vel_out, str_out, mem_out, held, load_sem, store_sem):
+    rows = [(src.at[i], dst.at[i]) for src, dst in ((mem_in, mem_out), (str_in, str_out), (vel_in, vel_out))
+            for i in range(src.shape[0])]
+    loads = [
+        pltpu.make_async_copy(src, held.at[i], load_sem.at[i]) for i, (src, dst) in enumerate(rows)
+    ]
+    stores = [
+        pltpu.make_async_copy(held.at[i], dst, store_sem.at[i]) for i, (src, dst) in enumerate(rows)
+    ]
+    for copy in loads:
+        copy.start()
+    for load, store in zip(loads, stores):
+        load.wait()
+        store.start()
+    for copy in stores:
+        copy.wait()
+
+
 def on_device(depth_devices, az_devices, velocity, stress, memory, layer_ids, materials, jkd, source_depth):
     depth, azims, radii = velocity.shape[1:]
     chunks = depth // 4
@@ -670,7 +688,7 @@
     def held(*shape):
         return pltpu.VMEM(shape + plane, F32)
 
-    return tuple(pl.pallas_call(
+    results = pl.pallas_call(
         functools.partial(step_kernel, depth_devices, az_devices),
         out_shape=tuple(jax.ShapeDtypeStruct(x.shape, x.dtype) for x in (velocity, stress, memory)),
         in_specs=[smem] + [hbm] * 8,
@@ -718,7 +736,19 @@
             flops=10**9, bytes_accessed=2 * 25 * velocity.size // 6 * 4, transcendentals=0
         ),
         name="biot_steps",
-    )(source_depth, *small, velocity, stress, memory))
+    )(source_depth, *small, velocity, stress, memory)
+    return tuple(pl.pallas_call(
+        deliver_kernel,
+        out_shape=tuple(jax.ShapeDtypeStruct(x.shape, x.dtype) for x in results),
+        in_specs=[hbm] * 3,
+        out_specs=(hbm,) * 3,
+        scratch_shapes=[held(25, depth), dma((25,)), dma((25,))],
+        compiler_params=pltpu.CompilerParams(vmem_limit_bytes=64 * 1024 * 1024),
+        cost_estimate=pl.CostEstimate(
+            flops=0, bytes_accessed=2 * 25 * velocity.size // 6 * 4, transcendentals=0
+        ),
+        name="deliver",
+    )(*results))
 
 
 def solution(mesh):

time: 85.3 us -> 83.9 us (0.984)
  local copies, waits for them, and re-layouts: 7.11 us -> 0 us
  Pallas kernels: 76.7 us -> 82.4 us
    unnamed x7 -> x0, local copies, waits for them, and re-layouts: 7.11 us -> none
    pallas_call x0 -> x1, Pallas kernels: none -> 5.66 us  [on_device(): pl.pallas_call(deliver_kernel, out_shape=tuple((jax.ShapeDtypeStruct(x.sh...]
where the time goes in v3:
time: 83.9 us; the launch traced here: 83.7 us
  Pallas kernels  82.4 us (98%)
  between operations  1.29 us (2%)
    pallas_call x1, Pallas kernels, on_device(): pl.pallas_call(functools.partial(step_kernel, depth_devices, az_devices),...  76.8 us
    pallas_call x1, Pallas kernels, on_device(): pl.pallas_call(deliver_kernel, out_shape=tuple((jax.ShapeDtypeStruct(x.sh...  5.66 us

profile of v3, /device:TPU:0, one launch (start us, length us, event | category | flops | bytes accessed | tf_op | source)
XLA Modules:
  0.0 83.7 jit_solution(5415238864685174202)
XLA Ops:
  1.3 76.8 %biot_steps.1 = (f32[6,16,32,128]{3,2,1,0:T(8,128)}, f32[7,16,32,128]{3,2,1,0:T(8,128)}, f32[12,16,32,128]{3,2,1,0:T(8,128)}) custom-call(s32[1]{0:T(128)S(6)} %copy.12.source, f32[8,8]{1,0:T(8,128)} %mats_in.1, f32[8,9]{1,0:T(8,128)} %jkd_in.1, s32[4,32]{1,0:T(4,128)} %ids_in.1, bf16[384,128]{1,0:T(8,128)(2,1)} %constant.4.clone.radial_in, ...), custom_call_target="tpu_custom_call" | custom-call | flops 1000000000 | bytes 13107200 | tf_op jit(solution)/shard_map/biot_steps/pallas_call | solution.py:691
  78.0 5.7 %deliver.1 = (f32[6,16,32,128]{3,2,1,0:T(8,128)}, f32[7,16,32,128]{3,2,1,0:T(8,128)}, f32[12,16,32,128]{3,2,1,0:T(8,128)}) custom-call(f32[6,16,32,128]{3,2,1,0:T(8,128)} %get-tuple-element.6.vel_in, f32[7,16,32,128]{3,2,1,0:T(8,128)} %get-tuple-element.7.str_in, f32[12,16,32,128]{3,2,1,0:T(8,128)} %get-tuple-element.8.mem_in), custom_call_target="tpu_custom_call" | custom-call | bytes 13107200 | tf_op jit(solution)/shard_map/deliver/pallas_call | solution.py:740

commit v4 on v3

--- a/solution.py
+++ b/solution.py
@@ -81,7 +81,7 @@
     mem, inv_r, s_az, s_rest, v_az, v_rest, far_s, far_v, far_new, far_dw, far_psi, far_dt, dw, psi_t,
     halo_above, halo_below, far_above, far_below, up_stage, down_stage,
     partial, far_partial, coef, rad_d, az_d,
-    load_sem, store_sem, chunk_sem, az_send, az_recv, up_send, up_recv, down_send, down_recv,
+    load_sem, first_sem, store_sem, chunk_sem, az_send, az_recv, up_send, up_recv, down_send, down_recv,
 ):
     me_d = lax.axis_index("depth")
     me_a = lax.axis_index("az")
@@ -103,7 +103,19 @@
     loads = [
         pltpu.make_async_copy(src, dst, load_sem.at[i]) for i, (src, dst) in enumerate(pairs)
     ]
-    for index in (1, 3, 5, 6, 14, 15, 16, 0, 2, 4, 17, 18, 7, 8, 9, 10, 11, 12, 13):
+    order = [0] + ([chunks - 1] if chunks > 1 else []) + list(range(1, chunks - 1))
+
+    def first_loads(e):
+        planes = pl.ds(4 * e, 4)
+        return [
+            pltpu.make_async_copy(str_in.at[i, planes], s_az.at[k, planes], first_sem.at[e, k])
+            for k, i in enumerate((3, 1, 5, 6))
+        ]
+
+    for e in order:
+        for copy in first_loads(e):
+            copy.start()
+    for index in (14, 15, 16, 0, 2, 4, 17, 18, 7, 8, 9, 10, 11, 12, 13):
         loads[index].start()
 
     def other_az(k, sign):
@@ -482,10 +494,9 @@
 
         lax.fori_loop(0, chunks, wrapped, 0)
 
-    for index in (1, 3, 5, 6):
-        loads[index].wait()
-    order = [0] + ([chunks - 1] if chunks > 1 else []) + list(range(1, chunks - 1))
     for e in order:
+        for copy in first_loads(e):
+            copy.wait()
         start_az(0, e)
     for index in (0, 2, 4):
         loads[index].wait()
@@ -720,6 +731,7 @@
             held(4, 4),
             pltpu.VMEM((4, azims, 4 * radii), F32),
             dma((19,)),
+            dma((chunks, 4)),
             dma((7,)),
             dma((chunks, 7)),
             dma((5, others, chunks)),

time: 83.9 us -> 84 us (level)
  no operation moved by 1% of the time
where the time goes in v4:
time: 84 us; the launch traced here: 83.8 us
  Pallas kernels  82.5 us (98%)
  between operations  1.29 us (2%)
    pallas_call x1, Pallas kernels, on_device(): pl.pallas_call(functools.partial(step_kernel, depth_devices, az_devices),...  76.8 us
    pallas_call x1, Pallas kernels, on_device(): pl.pallas_call(deliver_kernel, out_shape=tuple((jax.ShapeDtypeStruct(x.sh...  5.66 us

profile of v4, /device:TPU:0, one launch (start us, length us, event | category | flops | bytes accessed | tf_op | source)
XLA Modules:
  0.0 83.8 jit_solution(8848771167740057232)
XLA Ops:
  1.3 76.8 %biot_steps.1 = (f32[6,16,32,128]{3,2,1,0:T(8,128)}, f32[7,16,32,128]{3,2,1,0:T(8,128)}, f32[12,16,32,128]{3,2,1,0:T(8,128)}) custom-call(s32[1]{0:T(128)S(6)} %copy.12.source, f32[8,8]{1,0:T(8,128)} %mats_in.1, f32[8,9]{1,0:T(8,128)} %jkd_in.1, s32[4,32]{1,0:T(4,128)} %ids_in.1, bf16[384,128]{1,0:T(8,128)(2,1)} %constant.4.clone.radial_in, ...), custom_call_target="tpu_custom_call" | custom-call | flops 1000000000 | bytes 13107200 | tf_op jit(solution)/shard_map/biot_steps/pallas_call | solution.py:702
  78.1 5.7 %deliver.1 = (f32[6,16,32,128]{3,2,1,0:T(8,128)}, f32[7,16,32,128]{3,2,1,0:T(8,128)}, f32[12,16,32,128]{3,2,1,0:T(8,128)}) custom-call(f32[6,16,32,128]{3,2,1,0:T(8,128)} %get-tuple-element.6.vel_in, f32[7,16,32,128]{3,2,1,0:T(8,128)} %get-tuple-element.7.str_in, f32[12,16,32,128]{3,2,1,0:T(8,128)} %get-tuple-element.8.mem_in), custom_call_target="tpu_custom_call" | custom-call | bytes 13107200 | tf_op jit(solution)/shard_map/deliver/pallas_call | solution.py:752
